TPU v7x, 512 devices: a whole 4x4x16 slice. The times are simulated.
512 devices in a mesh: leaf: 16 (over z), panel: 32 (over y, x, core).
Axes of the slice: x: 4, y: 4, z: 16, core: 2. Of those that a mesh axis runs over, the one named last changes fastest.
Arguments:
- probe_low: bfloat16 [16, 4096, 256], P('leaf', 'panel'), may hold values from -6 to 6
- probe_mid: bfloat16 [16, 2048, 256], P('leaf', 'panel'), may hold values from -6 to 6
- probe_top: bfloat16 [16, 1024, 256], P('leaf', 'panel'), may hold values from -6 to 6
- inv_low: bfloat16 [16, 4096, 4096], P('leaf', 'panel'), may hold values from -0.09375 to 0.09375
- inv_mid: bfloat16 [16, 2048, 4096], P('leaf', 'panel'), may hold values from -0.09375 to 0.09375
- inv_top: bfloat16 [16, 1024, 4096], P('leaf', 'panel'), may hold values from -0.09375 to 0.09375
- gram_low: bfloat16 [16, 4096, 4096], P('leaf', 'panel'), may hold values from -0.09375 to 0.09375
- gram_mid: bfloat16 [16, 2048, 4096], P('leaf', 'panel'), may hold values from -0.09375 to 0.09375
- gram_top: bfloat16 [16, 1024, 4096], P('leaf', 'panel'), may hold values from -0.09375 to 0.09375
- panel_low: bfloat16 [16, 1024, 4096], P('leaf', 'panel'), may hold values from -0.09375 to 0.09375
- panel_mid: bfloat16 [16, 512, 4096], P('leaf', 'panel'), may hold values from -0.09375 to 0.09375
- back_low: bfloat16 [16, 4096, 1024], P('leaf', 'panel'), may hold values from -0.1875 to 0.1875
- back_mid: bfloat16 [16, 2048, 1024], P('leaf', 'panel'), may hold values from -0.1875 to 0.1875
- sep_low: int32 [16, 1024], replicated, may hold values from 0 to 4095, as said below
- sep_mid: int32 [8, 1024], replicated, may hold values from 0 to 4095, as said below
Outputs:
- half_low: bfloat16 [16, 4096, 256], P('leaf', 'panel')
- half_mid: bfloat16 [16, 2048, 256], P('leaf', 'panel')
- half_top: bfloat16 [16, 1024, 256], P('leaf', 'panel')
- solved_low: bfloat16 [16, 4096, 256], P('leaf', 'panel')
- solved_mid: bfloat16 [16, 2048, 256], P('leaf', 'panel')
- solved_top: bfloat16 [16, 1024, 256], P('leaf', 'panel')
Inputs may be any that keep to these rules, and one draw needn't show every extreme that they name: Each row of sep_low lists 1024 distinct rows of a parent supernode; 0 and 4095 occur in every row. Each row of sep_mid lists 1024 distinct rows of a parent supernode; 0 and 4095 occur in every row.
All inputs are finite; a program needn't handle non-finite values.
Results may differ from a plain program's by a relative error of at most 0.0085.
Values may be sent and summed in bfloat16 or wider, within the bound.
A program may use at most 64 MiB of HBM per device.

v0:
```python
import jax
import jax.numpy as jnp
from jax import lax
from jax.sharding import PartitionSpec as P


def from_partner(value, axis, bit):
    mask = 2**bit
    pairs = [(source, source ^ mask) for source in range(lax.axis_size(axis))]
    return lax.ppermute(value, axis, pairs)


def pair_up(block, bit):
    partner = from_partner(block, "leaf", bit)
    upper = lax.axis_index("leaf") >> bit & 1 == 1
    return jnp.where(
        upper, jnp.concatenate([partner, block], 0), jnp.concatenate([block, partner], 0)
    )


def sibling(block, bit):
    return from_partner(block, "leaf", bit)


def collect(piece, depth):
    whole = lax.all_gather(piece, "panel", axis=1, tiled=True)
    for bit in range(depth):
        whole = pair_up(whole, bit)
    return whole.reshape(-1, whole.shape[-1])


def product(matrix, rhs):
    return jnp.dot(matrix[0], rhs, preferred_element_type=jnp.float32)


def own_rows(full, depth, count):
    block = lax.axis_index("leaf") & (1 << depth) - 1
    start = (block * lax.axis_size("panel") + lax.axis_index("panel")) * count
    return lax.dynamic_slice_in_dim(full, start, count, 0)


def child_total(updates, other, rows_table, depth, height):
    child = lax.axis_index("leaf") >> depth
    own_map = lax.dynamic_index_in_dim(rows_table, child, 0, keepdims=False)
    other_map = lax.dynamic_index_in_dim(rows_table, child ^ 1, 0, keepdims=False)
    total = jnp.zeros((height, updates.shape[1]), jnp.float32)
    total = total.at[own_map].add(updates.astype(jnp.float32))
    return total.at[other_map].add(other.astype(jnp.float32))


def parent_side(updates, other, rows_table, depth, probe_local):
    count = probe_local.shape[1]
    total = child_total(
        updates, other, rows_table, depth, count * lax.axis_size("panel") * (2 << depth)
    )
    local = probe_local[0].astype(jnp.float32) - own_rows(total, depth + 1, count)
    return local.astype(jnp.bfloat16)[None]


def sweeps(
    probe_low,
    probe_mid,
    probe_top,
    inv_low,
    inv_mid,
    inv_top,
    gram_low,
    gram_mid,
    gram_top,
    panel_low,
    panel_mid,
    back_low,
    back_mid,
    sep_low,
    sep_mid,
):
    leaf_index = lax.axis_index("leaf")
    right_low = collect(probe_low, 0)
    update_low = product(panel_low, right_low).astype(jnp.bfloat16)
    update_low = collect(update_low[None], 0)
    right_mid = collect(parent_side(update_low, sibling(update_low, 0), sep_low, 0, probe_mid), 1)
    update_mid = product(panel_mid, right_mid).astype(jnp.bfloat16)
    update_mid = collect(update_mid[None], 1)
    right_top = collect(parent_side(update_mid, sibling(update_mid, 1), sep_mid, 1, probe_top), 2)
    half_low = product(inv_low, right_low).astype(jnp.bfloat16)
    half_mid = product(inv_mid, right_mid).astype(jnp.bfloat16)
    half_top = product(inv_top, right_top).astype(jnp.bfloat16)
    solved_top = product(gram_top, right_top).astype(jnp.bfloat16)
    parent_top = collect(solved_top[None], 2)
    map_mid = lax.dynamic_index_in_dim(sep_mid, leaf_index >> 1, 0, keepdims=False)
    taken_mid = jnp.take(parent_top, map_mid, axis=0)
    solved_mid = (product(gram_mid, right_mid) - product(back_mid, taken_mid)).astype(jnp.bfloat16)
    parent_mid = collect(solved_mid[None], 1)
    map_low = lax.dynamic_index_in_dim(sep_low, leaf_index, 0, keepdims=False)
    taken_low = jnp.take(parent_mid, map_low, axis=0)
    solved_low = (product(gram_low, right_low) - product(back_low, taken_low)).astype(jnp.bfloat16)
    return (
        half_low[None],
        half_mid[None],
        half_top[None],
        solved_low[None],
        solved_mid[None],
        solved_top[None],
    )


def body(
    probe_low,
    probe_mid,
    probe_top,
    inv_low,
    inv_mid,
    inv_top,
    gram_low,
    gram_mid,
    gram_top,
    panel_low,
    panel_mid,
    back_low,
    back_mid,
    sep_low,
    sep_mid,
):
    blocks_rest = (
        inv_low,
        inv_mid,
        inv_top,
        gram_low,
        gram_mid,
        gram_top,
        panel_low,
        panel_mid,
        back_low,
        back_mid,
        sep_low,
        sep_mid,
    )
    return sweeps(probe_low, probe_mid, probe_top, *blocks_rest)


def solution(mesh):
    return jax.shard_map(
        body,
        mesh=mesh,
        in_specs=(
            P("leaf", "panel", None),
            P("leaf", "panel", None),
            P("leaf", "panel", None),
            P("leaf", "panel", None),
            P("leaf", "panel", None),
            P("leaf", "panel", None),
            P("leaf", "panel", None),
            P("leaf", "panel", None),
            P("leaf", "panel", None),
            P("leaf", "panel", None),
            P("leaf", "panel", None),
            P("leaf", "panel", None),
            P("leaf", "panel", None),
            P(),
            P(),
        ),
        out_specs=(
            P("leaf", "panel", None),
            P("leaf", "panel", None),
            P("leaf", "panel", None),
            P("leaf", "panel", None),
            P("leaf", "panel", None),
            P("leaf", "panel", None),
        ),
        check_vma=False,
    )
```

profile of v0, /device:TPU:1, one launch (start us, length us, event | category | flops | bytes accessed | tf_op | source)
XLA Modules:
  0.0 584.4 jit_solution(5055272088833783193)
XLA Ops:
  7.2 0.0 copy-start
  7.2 0.0 all-gather.10.cloned.1.call-start
  7.2 0.7 all-gather.10.cloned.1.call-update
  7.9 0.0 all-gather.12.cloned.1.call-start
  8.0 68.1 %all-gather.10.cloned.1.call-done = bf16[1,4096,256]{2,1,0:T(8,128)(2,1)} async-done(((bf16[1,128,256]{2,1,0:T(8,128)(2,1)}), bf16[1,4096,256]{2,1,0:T(8,128)(2,1)}) %all-gather.10.cloned.1.call-update) | async-done | bytes 2097168 | tf_op jit(solution)/shard_map/all_gather | solution.py:26
  76.1 2.1 fusion.21
  78.2 24.0 %all-gather = bf16[1024,256]{1,0:T(8,128)(2,1)S(1)} all-gather(bf16[32,256]{1,0:T(8,128)(2,1)S(1)} %fusion.21), channel_id=2, replica_groups=mesh['leaf'=16,'panel'=32] {'panel'}, dimensions={0}, use_global_device_ids=true | all-gather | bytes 540672 | tf_op jit(solution)/shard_map/all_gather | solution.py:26
  102.2 3.2 collective-permute-start
  105.4 0.9 compare_select_fusion.2
  106.3 8.3 %scatter_custom_fusion = f32[4096,256]{1,0:T(8,128)} fusion(s32[1024]{0:T(1024)S(1)} %bitcast.132, f32[]{:T(128)} %constant.45.clone.1, bf16[1024,256]{1,0:T(8,128)(2,1)S(1)} %all-gather), kind=kCustom, calls=%fused_computation.18 | custom fusion | flops 524288 | bytes 4718596 | tf_op jit(solution)/shard_map/scatter-add | solution.py:47
  114.6 2.9 collective-permute-done
  117.5 10.2 %scatter_custom_fusion.1 = f32[4096,256]{1,0:T(8,128)} fusion(f32[4096,256]{1,0:T(8,128)} %scatter_custom_fusion, s32[1024]{0:T(1024)S(1)} %bitcast.131, bf16[1024,256]{1,0:T(8,128)(2,1)S(1)} %collective-permute-done), kind=kCustom, calls=%fused_computation.43 | custom fusion | flops 524288 | bytes 4718592 | tf_op jit(solution)/shard_map/scatter-add | solution.py:48
  127.7 1.5 fusion.49
  129.2 0.0 all-gather.12.cloned.1.call-update
  129.2 0.0 all-gather.14.cloned.1.call-start
  129.2 57.7 %all-gather.12.cloned.1.call-done = bf16[2048,256]{1,0:T(8,128)(2,1)} async-done(((bf16[64,256]{1,0:T(8,128)(2,1)}), bf16[2048,256]{1,0:T(8,128)(2,1)}) %all-gather.12.cloned.1.call-update) | async-done | bytes 1048592 | tf_op jit(solution)/shard_map/all_gather | solution.py:26
  186.9 3.2 collective-permute-start.1
  190.1 23.5 %collective-permute-done.1 = bf16[1,2048,256]{2,1,0:T(8,128)(2,1)} collective-permute-done((bf16[1,2048,256]{2,1,0:T(8,128)(2,1)}, bf16[1,2048,256]{2,1,0:T(8,128)(2,1)}, u32[]{:S(2)}, u32[]{:S(2)}) %collective-permute-start.1) | collective-permute-done | bytes 1048608 | tf_op jit(solution)/shard_map/ppermute | solution.py:10
  213.6 2.6 maximum_select_fusion
  216.2 0.4 fusion.25
  216.6 24.9 %all-gather.2 = bf16[512,256]{1,0:T(8,128)(2,1)S(1)} all-gather(bf16[16,256]{1,0:T(8,128)(2,1)S(1)} %fusion.25), channel_id=4, replica_groups=mesh['leaf'=16,'panel'=32] {'panel'}, dimensions={0}, use_global_device_ids=true | all-gather | bytes 270336 | tf_op jit(solution)/shard_map/all_gather | solution.py:26
  241.6 3.2 collective-permute-start.2
  244.8 6.5 %collective-permute-done.2 = bf16[1,512,256]{2,1,0:T(8,128)(2,1)S(1)} collective-permute-done((bf16[1,512,256]{2,1,0:T(8,128)(2,1)S(1)}, bf16[1,512,256]{2,1,0:T(8,128)(2,1)S(1)}, u32[]{:S(2)}, u32[]{:S(2)}) %collective-permute-start.2) | collective-permute-done | bytes 262176 | tf_op jit(solution)/shard_map/ppermute | solution.py:10
  251.2 0.9 maximum_select_fusion.6
  252.1 4.3 collective-permute-start.3
  256.4 0.9 compare_select_fusion.1
  257.3 8.1 %scatter_custom_fusion.2 = f32[4096,256]{1,0:T(8,128)} fusion(s32[1024]{0:T(1024)S(1)} %bitcast.134, f32[]{:T(128)} %constant.45.clone.1, bf16[1024,256]{1,0:T(8,128)(2,1)} %bitcast.20), kind=kCustom, calls=%fused_computation.16 | custom fusion | flops 524288 | bytes 4718596 | tf_op jit(solution)/shard_map/scatter-add | solution.py:47
  265.4 13.8 %collective-permute-done.3 = bf16[1024,256]{1,0:T(8,128)(2,1)} collective-permute-done((bf16[1024,256]{1,0:T(8,128)(2,1)}, bf16[1024,256]{1,0:T(8,128)(2,1)}, u32[]{:S(2)}, u32[]{:S(2)}) %collective-permute-start.3) | collective-permute-done | bytes 524320 | tf_op jit(solution)/shard_map/ppermute | solution.py:10
  279.2 10.6 %scatter_custom_fusion.3 = f32[4096,256]{1,0:T(8,128)} fusion(f32[4096,256]{1,0:T(8,128)} %scatter_custom_fusion.2, s32[1024]{0:T(1024)S(1)} %bitcast.133, bf16[1024,256]{1,0:T(8,128)(2,1)} %collective-permute-done.3), kind=kCustom, calls=%fused_computation.40 | custom fusion | flops 524288 | bytes 4718592 | tf_op jit(solution)/shard_map/scatter-add | solution.py:48
  289.8 0.8 fusion.50
  290.6 24.0 %all-gather.3 = bf16[1024,256]{1,0:T(8,128)(2,1)S(1)} all-gather(bf16[32,256]{1,0:T(8,128)(2,1)S(1)} %fusion.50), channel_id=5, replica_groups=mesh['leaf'=16,'panel'=32] {'panel'}, dimensions={0}, use_global_device_ids=true | all-gather | bytes 540672 | tf_op jit(solution)/shard_map/all_gather | solution.py:26
  314.5 2.2 collective-permute-start.4
  316.8 13.0 %collective-permute-done.4 = bf16[1,1024,256]{2,1,0:T(8,128)(2,1)S(1)} collective-permute-done((bf16[1,1024,256]{2,1,0:T(8,128)(2,1)S(1)}, bf16[1,1024,256]{2,1,0:T(8,128)(2,1)S(1)}, u32[]{:S(2)}, u32[]{:S(2)}) %collective-permute-start.4) | collective-permute-done | bytes 524320 | tf_op jit(solution)/shard_map/ppermute | solution.py:10
  329.8 1.2 maximum_select_fusion.4
  330.9 4.1 collective-permute-start.5
  335.1 45.6 %collective-permute-done.5 = bf16[2,1024,256]{2,1,0:T(8,128)(2,1)} collective-permute-done((bf16[2,1024,256]{2,1,0:T(8,128)(2,1)}, bf16[2,1024,256]{2,1,0:T(8,128)(2,1)}, u32[]{:S(2)}, u32[]{:S(2)}) %collective-permute-start.5) | collective-permute-done | bytes 1048608 | tf_op jit(solution)/shard_map/ppermute | solution.py:10
  380.7 2.6 maximum_select_fusion.1
  383.3 0.5 convolution_convert_fusion.1
  383.8 0.0 copy-start.10
  383.8 25.3 %all-gather.4 = bf16[1024,256]{1,0:T(8,128)(2,1)S(1)} all-gather(bf16[32,256]{1,0:T(8,128)(2,1)S(1)} %bitcast.125), channel_id=6, replica_groups=mesh['leaf'=16,'panel'=32] {'panel'}, dimensions={0}, use_global_device_ids=true | all-gather | bytes 540672 | tf_op jit(solution)/shard_map/all_gather | solution.py:26
  409.1 2.2 collective-permute-start.6
  411.3 13.1 %collective-permute-done.6 = bf16[1,1024,256]{2,1,0:T(8,128)(2,1)S(1)} collective-permute-done((bf16[1,1024,256]{2,1,0:T(8,128)(2,1)S(1)}, bf16[1,1024,256]{2,1,0:T(8,128)(2,1)S(1)}, u32[]{:S(2)}, u32[]{:S(2)}) %collective-permute-start.6) | collective-permute-done | bytes 524320 | tf_op jit(solution)/shard_map/ppermute | solution.py:10
  424.3 0.2 maximum_select_fusion.5
  424.5 4.1 collective-permute-start.7
  428.6 45.4 %collective-permute-done.7 = bf16[2,1024,256]{2,1,0:T(8,128)(2,1)S(1)} collective-permute-done((bf16[2,1024,256]{2,1,0:T(8,128)(2,1)S(1)}, bf16[2,1024,256]{2,1,0:T(8,128)(2,1)S(1)}, u32[]{:S(2)}, u32[]{:S(2)}) %collective-permute-start.7) | collective-permute-done | bytes 1048608 | tf_op jit(solution)/shard_map/ppermute | solution.py:10
  474.0 1.6 maximum_select_fusion.2
  475.7 6.5 %gather_fusion = bf16[1024,256]{1,0:T(8,128)(2,1)} fusion(bf16[4096,256]{1,0:T(8,128)(2,1)} %bitcast.111, s32[1024]{0:T(1024)S(1)} %fusion.51), kind=kCustom, calls=%fused_computation.clone | custom fusion | bytes 1052672 | tf_op jit(solution)/shard_map/jit(_take)/gather | solution.py:91
  482.1 1.4 fusion.37
  483.5 2.1 fusion.19
  485.7 0.0 all-gather.14.cloned.1.call-update
  485.7 0.8 constant_dynamic-slice_fusion
  486.5 57.2 %all-gather.14.cloned.1.call-done = bf16[2048,256]{1,0:T(8,128)(2,1)} async-done(((bf16[64,256]{1,0:T(8,128)(2,1)}), bf16[2048,256]{1,0:T(8,128)(2,1)}) %all-gather.14.cloned.1.call-update) | async-done | bytes 1048592 | tf_op jit(solution)/shard_map/all_gather | solution.py:26
  543.6 3.4 collective-permute-start.8
  547.1 2.7 fusion.16
  549.8 0.4 fusion
  550.2 0.6 copy-done.6
  550.8 1.1 fusion.20
  551.9 0.5 copy-done.3
  552.4 1.1 fusion.24
  553.5 17.0 %collective-permute-done.8 = bf16[1,2048,256]{2,1,0:T(8,128)(2,1)S(1)} collective-permute-done((bf16[1,2048,256]{2,1,0:T(8,128)(2,1)}, bf16[1,2048,256]{2,1,0:T(8,128)(2,1)S(1)}, u32[]{:S(2)}, u32[]{:S(2)}) %collective-permute-start.8) | collective-permute-done | bytes 1048608 | tf_op jit(solution)/shard_map/ppermute | solution.py:10
  570.5 0.3 maximum_select_fusion.3
  570.9 0.0 copy-start.13
  570.9 4.9 gather_fusion.1
  575.8 2.1 fusion.15
  (29 shorter events, 0.1 us)
Async XLA Ops:
  7.2 539.9 %copy-start = (bf16[1,128,4096]{2,1,0:T(8,128)(2,1)S(1)}, bf16[1,128,4096]{2,1,0:T(8,128)(2,1)}, u32[]{:S(2)}) copy-start(bf16[1,128,4096]{2,1,0:T(8,128)(2,1)} %param.20) | copy-start | bytes 3145732
  7.2 68.9 %all-gather.10.cloned.1.call-start = ((), (), s32[]{:S(2)}) async-start(), calls=%async_computation | async-start | bytes 2162688 | tf_op jit(solution)/shard_map/all_gather | solution.py:26
  7.9 179.0 %all-gather.12.cloned.1.call-start = ((), (), s32[]{:S(2)}) async-start(), calls=%async_computation.1 | async-start | bytes 1081344 | tf_op jit(solution)/shard_map/all_gather | solution.py:26
  102.2 15.3 %collective-permute-start = (bf16[1024,256]{1,0:T(8,128)(2,1)S(1)}, bf16[1024,256]{1,0:T(8,128)(2,1)S(1)}, u32[]{:S(2)}, u32[]{:S(2)}) collective-permute-start(bf16[1024,256]{1,0:T(8,128)(2,1)S(1)} %all-gather), channel_id=1, source_target_pairs={{0,32},{32,0},{64,96},{96,64},{128,160},{160,128},{192,224},{224,1... | collective-permute-start | bytes 1572872 | tf_op jit(solution)/shard_map/ppermute | solution.py:10
  117.5 10.2 %copy-start.11 = (bf16[1,64,256]{2,1,0:T(8,128)(2,1)S(1)}, bf16[1,64,256]{2,1,0:T(8,128)(2,1)}, u32[]{:S(2)}) copy-start(bf16[1,64,256]{2,1,0:T(8,128)(2,1)} %param.18) | copy-start | bytes 98308
  129.2 414.4 %all-gather.14.cloned.1.call-start = ((), (), s32[]{:S(2)}) async-start(), calls=%async_computation.2 | async-start | bytes 1081344 | tf_op jit(solution)/shard_map/all_gather | solution.py:26
  186.9 26.7 %collective-permute-start.1 = (bf16[1,2048,256]{2,1,0:T(8,128)(2,1)}, bf16[1,2048,256]{2,1,0:T(8,128)(2,1)}, u32[]{:S(2)}, u32[]{:S(2)}) collective-permute-start(bf16[1,2048,256]{2,1,0:T(8,128)(2,1)} %bitcast.119), channel_id=1, source_target_pairs={{0,32},{32,0},{64,96},{96,64},{128,160},{160,128},{192,224},{224,1... | collective-permute-start | bytes 3145736 | tf_op jit(solution)/shard_map/ppermute | solution.py:10
  190.1 26.2 %copy-start.9 = (bf16[1,16,4096]{2,1,0:T(8,128)(2,1)S(1)}, bf16[1,16,4096]{2,1,0:T(8,128)(2,1)}, u32[]{:S(2)}) copy-start(bf16[1,16,4096]{2,1,0:T(8,128)(2,1)} %param.27) | copy-start | bytes 393220
  241.6 9.6 %collective-permute-start.2 = (bf16[1,512,256]{2,1,0:T(8,128)(2,1)S(1)}, bf16[1,512,256]{2,1,0:T(8,128)(2,1)S(1)}, u32[]{:S(2)}, u32[]{:S(2)}) collective-permute-start(bf16[1,512,256]{2,1,0:T(8,128)(2,1)S(1)} %bitcast.121), channel_id=1, source_target_pairs={{0,32},{32,0},{64,96},{96,64},{128,160},{160,128},{192,224},{224,1... | collective-permute-start | bytes 786440 | tf_op jit(solution)/shard_map/ppermute | solution.py:10
  252.1 27.1 %collective-permute-start.3 = (bf16[1024,256]{1,0:T(8,128)(2,1)}, bf16[1024,256]{1,0:T(8,128)(2,1)}, u32[]{:S(2)}, u32[]{:S(2)}) collective-permute-start(bf16[1024,256]{1,0:T(8,128)(2,1)} %bitcast.20), channel_id=1, source_target_pairs={{0,64},{32,96},{64,0},{96,32},{128,192},{160,224},{192,128},{224,1... | collective-permute-start | bytes 1572872 | tf_op jit(solution)/shard_map/ppermute | solution.py:10
  279.2 10.6 %copy-start.12 = (bf16[1,32,256]{2,1,0:T(8,128)(2,1)S(1)}, bf16[1,32,256]{2,1,0:T(8,128)(2,1)}, u32[]{:S(2)}) copy-start(bf16[1,32,256]{2,1,0:T(8,128)(2,1)} %param.19) | copy-start | bytes 49156
  314.5 15.3 %collective-permute-start.4 = (bf16[1,1024,256]{2,1,0:T(8,128)(2,1)S(1)}, bf16[1,1024,256]{2,1,0:T(8,128)(2,1)S(1)}, u32[]{:S(2)}, u32[]{:S(2)}) collective-permute-start(bf16[1,1024,256]{2,1,0:T(8,128)(2,1)S(1)} %bitcast.113), channel_id=1, source_target_pairs={{0,32},{32,0},{64,96},{96,64},{128,160},{160,128},{192,224},{224,1... | collective-permute-start | bytes 1572872 | tf_op jit(solution)/shard_map/ppermute | solution.py:10
  330.9 49.8 %collective-permute-start.5 = (bf16[2,1024,256]{2,1,0:T(8,128)(2,1)}, bf16[2,1024,256]{2,1,0:T(8,128)(2,1)}, u32[]{:S(2)}, u32[]{:S(2)}) collective-permute-start(bf16[2,1024,256]{2,1,0:T(8,128)(2,1)} %maximum_select_fusion.4), channel_id=1, source_target_pairs={{0,64},{32,96},{64,0},{96,32},{128,192},{160,224},{192,128},{224,1... | collective-permute-start | bytes 3145736 | tf_op jit(solution)/shard_map/ppermute | solution.py:10
  335.1 48.3 %copy-start.7 = (bf16[1,32,4096]{2,1,0:T(8,128)(2,1)S(1)}, bf16[1,32,4096]{2,1,0:T(8,128)(2,1)}, u32[]{:S(2)}) copy-start(bf16[1,32,4096]{2,1,0:T(8,128)(2,1)} %param.25) | copy-start | bytes 786436
  383.3 41.2 %copy-start.2 = (bf16[4,1024,256]{2,1,0:T(8,128)(2,1)}, bf16[4,1024,256]{2,1,0:T(8,128)(2,1)S(1)}, u32[]{:S(2)}) copy-start(bf16[4,1024,256]{2,1,0:T(8,128)(2,1)S(1)} %maximum_select_fusion.1) | copy-start | bytes 6291460
  383.8 91.9 %copy-start.10 = (bf16[256,32]{0,1:T(8,128)(2,1)}, bf16[256,32]{0,1:T(8,128)(2,1)S(1)}, u32[]{:S(2)}) copy-start(bf16[256,32]{0,1:T(8,128)(2,1)S(1)} %convolution_convert_fusion.1) | copy-start | bytes 49156
  409.1 15.3 %collective-permute-start.6 = (bf16[1,1024,256]{2,1,0:T(8,128)(2,1)S(1)}, bf16[1,1024,256]{2,1,0:T(8,128)(2,1)S(1)}, u32[]{:S(2)}, u32[]{:S(2)}) collective-permute-start(bf16[1,1024,256]{2,1,0:T(8,128)(2,1)S(1)} %bitcast.115), channel_id=1, source_target_pairs={{0,32},{32,0},{64,96},{96,64},{128,160},{160,128},{192,224},{224,1... | collective-permute-start | bytes 1572872 | tf_op jit(solution)/shard_map/ppermute | solution.py:10
  424.5 49.5 %collective-permute-start.7 = (bf16[2,1024,256]{2,1,0:T(8,128)(2,1)S(1)}, bf16[2,1024,256]{2,1,0:T(8,128)(2,1)S(1)}, u32[]{:S(2)}, u32[]{:S(2)}) collective-permute-start(bf16[2,1024,256]{2,1,0:T(8,128)(2,1)S(1)} %maximum_select_fusion.5), channel_id=1, source_target_pairs={{0,64},{32,96},{64,0},{96,32},{128,192},{160,224},{192,128},{224,1... | collective-permute-start | bytes 3145736 | tf_op jit(solution)/shard_map/ppermute | solution.py:10
  475.7 6.5 %copy-start.14 = (bf16[1,64,1024]{2,1,0:T(8,128)(2,1)S(1)}, bf16[1,64,1024]{2,1,0:T(8,128)(2,1)}, u32[]{:S(2)}) copy-start(bf16[1,64,1024]{2,1,0:T(8,128)(2,1)} %param.29) | copy-start | bytes 393220
  543.6 6.1 %copy-start.1 = (bf16[1,4096,256]{2,1,0:T(8,128)(2,1)S(1)}, bf16[1,4096,256]{2,1,0:T(8,128)(2,1)}, u32[]{:S(2)}) copy-start(bf16[1,4096,256]{2,1,0:T(8,128)(2,1)} %all-gather.10.cloned.1.call-done) | copy-start | bytes 6291460
  543.6 6.1 %copy-start.4 = (bf16[1,128,4096]{2,1,0:T(8,128)(2,1)S(1)}, bf16[1,128,4096]{2,1,0:T(8,128)(2,1)}, u32[]{:S(2)}) copy-start(bf16[1,128,4096]{2,1,0:T(8,128)(2,1)} %param.23) | copy-start | bytes 3145732
  543.6 26.9 %collective-permute-start.8 = (bf16[1,2048,256]{2,1,0:T(8,128)(2,1)}, bf16[1,2048,256]{2,1,0:T(8,128)(2,1)S(1)}, u32[]{:S(2)}, u32[]{:S(2)}) collective-permute-start(bf16[1,2048,256]{2,1,0:T(8,128)(2,1)} %bitcast.117), channel_id=1, source_target_pairs={{0,32},{32,0},{64,96},{96,64},{128,160},{160,128},{192,224},{224,1... | collective-permute-start | bytes 3145736 | tf_op jit(solution)/shard_map/ppermute | solution.py:10
  549.8 1.0 copy-start.6
  549.8 2.1 copy-start.8
  550.8 1.6 copy-start.3
  550.8 19.7 %copy-start.5 = (bf16[2048,256]{1,0:T(8,128)(2,1)S(1)}, bf16[2048,256]{1,0:T(8,128)(2,1)}, u32[]{:S(2)}) copy-start(bf16[2048,256]{1,0:T(8,128)(2,1)} %all-gather.14.cloned.1.call-done) | copy-start | bytes 3145732
  570.9 5.0 copy-start.13
Sparse Core Ops, SparseCore 0:
  11.2 64.8 all-gather.9
  129.3 57.5 all-gather.11
  485.8 57.7 all-gather.13
where the time goes:
time: 585 us; the launch traced here: 584 us
  waiting for transfers between devices  364 us (62%)
  blocking collectives  98.2 us (17%)
  other arithmetic  50.5 us (9%)
  starting transfers between devices  30.1 us (5%)
  between operations  14 us (2%)
  matrix products  13.8 us (2%)
  local copies, waits for them, and re-layouts  13.4 us (2%)
    all_gather x3, waiting for transfers between devices, collect(): whole = lax.all_gather(piece, 'panel', axis=1, tiled=True)  183 us
    ppermute x9, waiting for transfers between devices, from_partner(): return lax.ppermute(value, axis, pairs)  181 us
    all_gather x4, blocking collectives, collect(): whole = lax.all_gather(piece, 'panel', axis=1, tiled=True)  98.2 us
    ppermute x9, starting transfers between devices, from_partner(): return lax.ppermute(value, axis, pairs)  29.9 us
    scatter-add x2, other arithmetic, child_total(): return total.at[other_map].add(other.astype(jnp.float32))  20.8 us
    scatter-add x2, other arithmetic, child_total(): total = total.at[own_map].add(updates.astype(jnp.float32))  16.4 us
    dot_general x10, matrix products, product(): return jnp.dot(matrix[0], rhs, preferred_element_type=jnp.float32)  13.8 us
  transfers between devices with their start and end apart: 12, of which 12 were waited for; matrix products, arithmetic and copies ran while one was open for 4% of the time, Pallas kernels for 0%

commit v1 on v0

v1 whole, which is shorter than its diff:
```python
import jax
import jax.numpy as jnp
from jax import lax
from jax.experimental import pallas as pl
from jax.experimental.pallas import tpu as pltpu
from jax.sharding import PartitionSpec as P

MESH = pl.DeviceIdType.MESH
BF16, F32 = jnp.bfloat16, jnp.float32
HALF = 128
RIGHT_LOW, UPDATE_LOW, UPDATE_MID, SOLVED_TOP, SOLVED_MID, PROBE_MID, PROBE_TOP = range(7)


def kernel(
    probe_low, probe_mid, probe_top, inv_low, inv_mid, inv_top, gram_low, gram_mid, gram_top,
    panel_low, panel_mid, back_low, back_mid, sep_low, sep_mid,
    half_low, half_mid, half_top, solved_low, solved_mid, solved_top,
    d_rl, d_ul, d_um, d_st, d_sm, d_pm, d_pt,
    m_pl, m_low, m_mid, m_top, b_low, b_mid, s_low, s_mid, onehot, onehot_t, high,
    q_mid, q_top, c_low, c_mid, acc_low, acc_mid, acc_top,
    o_hl, o_hm, o_ht, o_sl, o_sm, o_st,
    load_sem, out_sem, core_send, core_recv, send_sem, recv_sem,
):
    z = lax.axis_index("leaf")
    p = lax.axis_index("panel")
    c = lax.rem(p, 2)
    x = lax.rem(p // 2, 4)
    y = p // 8
    z2, z4 = lax.rem(z, 2), lax.rem(z, 4)
    cols = pl.ds(pl.multiple_of(c * HALF, HALF), HALF)
    other_cols = pl.ds(pl.multiple_of((1 - c) * HALF, HALF), HALF)

    def chip(xx, yy):
        return {"leaf": z, "panel": (yy * 4 + xx) * 2 + c}

    sibling = {"leaf": z, "panel": p + 1 - 2 * c}

    loads = []

    def load(src, dst):
        copy = pltpu.make_async_copy(src, dst, load_sem.at[len(loads)])
        copy.start()
        loads.append(copy)
        return copy

    def rows(count):
        return pl.ds(pl.multiple_of(c * count, count), count)

    own = [
        load(probe_low.at[0, :, cols], d_rl.at[0, y, x, rows(128)]),
        load(probe_mid.at[0, :, cols], d_pm.at[z2, y, x, rows(64)]),
        load(probe_top.at[0, :, cols], d_pt.at[z4, y, x, rows(32)]),
    ]
    load_sep = [load(sep_low, s_low), load(sep_mid, s_mid)]
    load_pl = load(panel_low.at[0], m_pl.at[c])
    load_mid = [
        load(panel_mid.at[0], m_mid.at[c, 0:16]),
        load(inv_mid.at[0], m_mid.at[c, 16:80]),
        load(gram_mid.at[0], m_mid.at[c, 80:144]),
    ]
    load_low = [load(inv_low.at[0], m_low.at[c, 0]), load(gram_low.at[0], m_low.at[c, 1])]
    load_top = [load(gram_top.at[0], m_top.at[c, 0:32]), load(inv_top.at[0], m_top.at[c, 32:64])]
    load_back = [load(back_low.at[0], b_low), load(back_mid.at[0], b_mid)]

    barrier = pltpu.get_barrier_semaphore()
    pl.semaphore_signal(barrier, 1, device_id=sibling, device_id_type=MESH)
    for d in (1, 2, 3):
        pl.semaphore_signal(barrier, 1, device_id=chip(x ^ d, y), device_id_type=MESH)
        pl.semaphore_signal(barrier, 1, device_id=chip(x, y ^ d), device_id_type=MESH)
        pl.semaphore_signal(barrier, 1, device_id={"leaf": z ^ d, "panel": p}, device_id_type=MESH)
    pl.semaphore_wait(barrier, 10)

    sent = []

    core_count = [0]

    def swap(src, dst, arriving):
        i = core_count[0]
        core_count[0] += 1
        copy = pltpu.make_async_remote_copy(
            src, dst, core_send.at[i], core_recv.at[i], device_id=sibling, device_id_type=MESH
        )
        copy.start()
        sent.append(copy)
        return pltpu.make_async_remote_copy(
            arriving, arriving, core_send.at[i], core_recv.at[i], device_id=sibling, device_id_type=MESH
        )

    def other(count):
        return pl.ds(pl.multiple_of((1 - c) * count, count), count)

    def swap_probe(src, buf, zz, n):
        return swap(
            src.at[0, :, other_cols], buf.at[zz, y, x, rows(n)], buf.at[zz, y, x, other(n)]
        )

    in_rl = swap_probe(probe_low, d_rl, 0, 128)
    in_pm = swap_probe(probe_mid, d_pm, z2, 64)
    in_pt = swap_probe(probe_top, d_pt, z4, 32)

    def swap_rows(src, buf, *place):
        return swap(src, buf.at[(c, *place)], buf.at[(1 - c, *place)])

    in_pl = swap_rows(panel_low.at[0], m_pl)

    def z_copy(buf, g, size, d):
        zz = lax.rem(z, size)

        def make(at):
            return pltpu.make_async_remote_copy(
                buf.at[at, y, x], buf.at[at, y, x], send_sem.at[g, 0, d - 1], recv_sem.at[g, 0, d - 1],
                device_id={"leaf": z ^ d, "panel": p}, device_id_type=MESH,
            )

        return make(zz), make(zz ^ d)

    def first_copy(buf, g, d):
        xd = jnp.where(c == 0, x ^ d, x)
        yd = jnp.where(c == 0, y, y ^ d)

        def make(xx, yy):
            return pltpu.make_async_remote_copy(
                buf.at[:, yy, xx], buf.at[:, yy, xx], send_sem.at[g, 1, d - 1], recv_sem.at[g, 1, d - 1],
                device_id=chip(xd, yd), device_id_type=MESH,
            )

        return make(x, y), make(xd, yd)

    def second_row(buf, g, d):
        def make(yy):
            return pltpu.make_async_remote_copy(
                buf.at[:, yy], buf.at[:, yy], send_sem.at[g, 2, d - 1], recv_sem.at[g, 2, d - 1],
                device_id=chip(x, y ^ d), device_id_type=MESH,
            )

        return make(y), make(y ^ d)

    def second_column(buf, g, d):
        def make(xx):
            return pltpu.make_async_remote_copy(
                buf.at[:, :, xx], buf.at[:, :, xx], send_sem.at[g, 2, d - 1], recv_sem.at[g, 2, d - 1],
                device_id=chip(x ^ d, y), device_id_type=MESH,
            )

        return make(x), make(x ^ d)

    def z_start(buf, g, size):
        for d in range(1, size):
            z_copy(buf, g, size, d)[0].start()

    def z_wait(buf, g, size):
        for d in range(1, size):
            out, arriving = z_copy(buf, g, size, d)
            arriving.wait_recv()
            out.wait_send()

    def first_start(buf, g):
        for d in (1, 3, 2):
            first_copy(buf, g, d)[0].start()

    def first_wait(buf, g):
        for d in (1, 3, 2):
            out, arriving = first_copy(buf, g, d)
            arriving.wait_recv()
            out.wait_send()

    def second(act):
        @pl.when(c == 0)
        def _():
            for d in (1, 3, 2):
                act(second_row, d)

        @pl.when(c == 1)
        def _():
            for d in (1, 3, 2):
                act(second_column, d)

    def second_start(buf, g):
        second(lambda make, d: make(buf, g, d)[0].start())

    def second_wait(buf, g):
        def act(make, d):
            out, arriving = make(buf, g, d)
            arriving.wait_recv()
            out.wait_send()

        second(act)

    def dot(a, b):
        return jnp.dot(a, b, preferred_element_type=F32)

    def whole(buf):
        return buf[...].reshape(-1, HALF)

    def tables():
        for i in range(4):
            table, row = (s_low, (z - z2) + i) if i < 2 else (s_mid, 2 * (z // 4) + i - 2)
            sep = table[pl.ds(row, 1), :]
            high[i : i + 1, :] = lax.shift_right_logical(sep, 8)
            low = jnp.bitwise_and(sep, 255)
            for j in range(4):
                at = slice(j * 256, (j + 1) * 256)
                grid = lax.broadcasted_iota(jnp.int32, (256, 256), 0)
                hot = jnp.where(grid == low[:, at], 1.0, 0.0)
                onehot[i, :, at] = hot.astype(BF16)

    def own_tables():
        for i, (table, row) in enumerate(((s_low, z), (s_mid, z // 2))):
            sep = table[pl.ds(row, 1), :]
            high[4 + i : 5 + i, :] = lax.shift_right_logical(sep, 8)
            low = jnp.bitwise_and(sep, 255)
            for j in range(4):
                at = slice(j * 256, (j + 1) * 256)
                grid = lax.broadcasted_iota(jnp.int32, (256, 256), 0)
                hot = jnp.where(grid == low[:, at], 1.0, 0.0)
                onehot_t[i, at, :] = hot.T.astype(BF16)

    def take_columns(src, dst, i, total, block):
        at0 = (i % 2) * 1024

        def step(r, _):
            part = pl.ds(pl.multiple_of(r * block, block), block)
            value = src[c, part, :]
            tall = jnp.concatenate([value[:, k * 256 : (k + 1) * 256] for k in range(16)], 0)
            for j in range(4):
                at = slice(j * 256, (j + 1) * 256)
                found = dot(tall, onehot[i, :, at])
                which = high[i : i + 1, at]
                picked = jnp.zeros((block, 256), F32)
                for k in range(16):
                    picked = jnp.where(which == k, found[k * block : (k + 1) * block], picked)
                dst[c, part, at0 + j * 256 : at0 + (j + 1) * 256] = picked.astype(BF16)
            return 0

        lax.fori_loop(0, total // block, step, 0)

    def spread_columns(src, dst, i, total, block):
        def step(r, _):
            part = pl.ds(pl.multiple_of(r * block, block), block)
            value = src[part, :]
            which = high[4 + i : 5 + i, :]
            tall = jnp.concatenate(
                [value * jnp.where(which == k, 1.0, 0.0).astype(BF16) for k in range(16)], 0
            )
            found = dot(tall, onehot_t[i])
            for k in range(16):
                dst[c, part, k * 256 : (k + 1) * 256] = found[k * block : (k + 1) * block].astype(BF16)
            return 0

        lax.fori_loop(0, total // block, step, 0)

    outs = []

    def give(out, buf):
        i = len(outs)
        copy = pltpu.make_async_copy(buf.at[c], out.at[0, :, cols], out_sem.at[i])
        copy.start()
        outs.append((copy, swap(buf.at[1 - c], out.at[0, :, cols], out.at[0, :, other_cols])))

    in_mid = [
        swap_rows(panel_mid.at[0], m_mid, slice(0, 16)),
        swap_rows(inv_mid.at[0], m_mid, slice(16, 80)),
        swap_rows(gram_mid.at[0], m_mid, slice(80, 144)),
    ]
    own[0].wait()
    in_rl.wait_recv()
    first_start(d_rl, RIGHT_LOW)
    own[1].wait()
    in_pm.wait_recv()
    z_start(d_pm, PROBE_MID, 2)
    own[2].wait()
    in_pt.wait_recv()
    z_start(d_pt, PROBE_TOP, 4)
    in_low = [
        swap_rows(inv_low.at[0], m_low, 0),
        swap_rows(gram_low.at[0], m_low, 1),
    ]
    in_top = [
        swap_rows(gram_top.at[0], m_top, slice(0, 32)),
        swap_rows(inv_top.at[0], m_top, slice(32, 64)),
    ]
    for copy in load_sep:
        copy.wait()
    tables()
    first_wait(d_rl, RIGHT_LOW)
    second_start(d_rl, RIGHT_LOW)
    z_wait(d_pm, PROBE_MID, 2)
    first_start(d_pm, PROBE_MID)
    for copy in load_mid:
        copy.wait()
    take_columns(m_mid, q_mid, 0, 144, 48)
    take_columns(m_mid, q_mid, 1, 144, 48)
    in_q_mid = swap_rows(q_mid.at[c], q_mid)
    load_pl.wait()
    in_pl.wait_recv()
    second_wait(d_rl, RIGHT_LOW)
    update = dot(m_pl[...].reshape(64, 4096), whole(d_rl))
    d_ul[z2, y, x] = update.astype(BF16)
    z_start(d_ul, UPDATE_LOW, 2)
    first_wait(d_pm, PROBE_MID)
    second_start(d_pm, PROBE_MID)
    own_tables()
    z_wait(d_ul, UPDATE_LOW, 2)
    first_start(d_ul, UPDATE_LOW)
    for copy in load_low:
        copy.wait()
    for copy in in_low:
        copy.wait_recv()
    result = dot(m_low[...].reshape(512, 4096), whole(d_rl)).reshape(2, 2, 128, HALF)
    o_hl[...] = result[:, 0].astype(BF16)
    acc_low[...] = result[:, 1]
    give(half_low, o_hl)
    first_wait(d_ul, UPDATE_LOW)
    second_start(d_ul, UPDATE_LOW)
    z_wait(d_pt, PROBE_TOP, 4)
    first_start(d_pt, PROBE_TOP)
    for copy in load_top:
        copy.wait()
    take_columns(m_top, q_top, 2, 64, 32)
    take_columns(m_top, q_top, 3, 64, 32)
    in_q_top = swap_rows(q_top.at[c], q_top)
    for copy in in_mid:
        copy.wait_recv()
    second_wait(d_pm, PROBE_MID)
    acc_mid[...] = dot(m_mid[...].reshape(288, 4096), whole(d_pm)).reshape(2, 144, HALF)
    in_q_mid.wait_recv()
    second_wait(d_ul, UPDATE_LOW)
    update = acc_mid[:, 0:16].reshape(32, HALF) - dot(q_mid[:, 0:16].reshape(32, 2048), whole(d_ul))
    d_um[z4, y, x] = update.astype(BF16)
    z_start(d_um, UPDATE_MID, 4)
    first_wait(d_pt, PROBE_TOP)
    second_start(d_pt, PROBE_TOP)
    result = acc_mid[:, 16:144] - dot(q_mid[:, 16:144].reshape(256, 2048), whole(d_ul)).reshape(2, 128, HALF)
    o_hm[...] = result[:, 0:64].astype(BF16)
    acc_mid[:, 16:144] = result
    give(half_mid, o_hm)
    z_wait(d_um, UPDATE_MID, 4)
    first_start(d_um, UPDATE_MID)
    for copy in load_back:
        copy.wait()
    spread_columns(b_mid, c_mid, 1, 64, 32)
    in_c_mid = swap_rows(c_mid.at[c], c_mid)
    first_wait(d_um, UPDATE_MID)
    second_start(d_um, UPDATE_MID)
    for copy in in_top:
        copy.wait_recv()
    second_wait(d_pt, PROBE_TOP)
    acc_top[...] = dot(m_top[...].reshape(128, 4096), whole(d_pt)).reshape(2, 64, HALF)
    in_q_top.wait_recv()
    second_wait(d_um, UPDATE_MID)
    result = acc_top[...] - dot(q_top[...].reshape(128, 2048), whole(d_um)).reshape(2, 64, HALF)
    top = result[:, 0:32].astype(BF16)
    d_st[z4, y, x] = top.reshape(64, HALF)
    z_start(d_st, SOLVED_TOP, 4)
    o_st[...] = top
    o_ht[...] = result[:, 32:64].astype(BF16)
    give(solved_top, o_st)
    give(half_top, o_ht)
    z_wait(d_st, SOLVED_TOP, 4)
    first_start(d_st, SOLVED_TOP)
    spread_columns(b_low, c_low, 0, 128, 32)
    in_c_low = swap_rows(c_low.at[c], c_low)
    first_wait(d_st, SOLVED_TOP)
    second_start(d_st, SOLVED_TOP)
    in_c_mid.wait_recv()
    second_wait(d_st, SOLVED_TOP)
    result = acc_mid[:, 80:144] - dot(c_mid[...].reshape(128, 4096), whole(d_st)).reshape(2, 64, HALF)
    mid = result.astype(BF16)
    d_sm[z2, y, x] = mid.reshape(128, HALF)
    z_start(d_sm, SOLVED_MID, 2)
    o_sm[...] = mid
    give(solved_mid, o_sm)
    z_wait(d_sm, SOLVED_MID, 2)
    first_start(d_sm, SOLVED_MID)
    first_wait(d_sm, SOLVED_MID)
    second_start(d_sm, SOLVED_MID)
    in_c_low.wait_recv()
    second_wait(d_sm, SOLVED_MID)
    result = acc_low[...] - dot(c_low[...].reshape(256, 4096), whole(d_sm)).reshape(2, 128, HALF)
    o_sl[...] = result.astype(BF16)
    give(solved_low, o_sl)
    for copy, arriving in outs:
        copy.wait()
        arriving.wait_recv()
    for copy in sent:
        copy.wait_send()


def body(*args):
    shapes = ((128, 0), (64, 1), (32, 2), (128, 0), (64, 1), (32, 2))

    def vmem(*shape, dtype=BF16):
        return pltpu.VMEM(shape, dtype)

    return pl.pallas_call(
        kernel,
        out_shape=tuple(jax.ShapeDtypeStruct((1, n, 256), BF16) for n, _ in shapes),
        in_specs=[pl.BlockSpec(memory_space=pl.ANY)] * 15,
        out_specs=tuple(pl.BlockSpec(memory_space=pl.ANY) for _ in shapes),
        scratch_shapes=[
            vmem(1, 4, 4, 256, HALF), vmem(2, 4, 4, 64, HALF), vmem(4, 4, 4, 32, HALF), vmem(4, 4, 4, 64, HALF),
            vmem(2, 4, 4, 128, HALF), vmem(2, 4, 4, 128, HALF), vmem(4, 4, 4, 64, HALF),
            vmem(2, 32, 4096), vmem(2, 2, 128, 4096), vmem(2, 144, 4096), vmem(2, 64, 4096),
            vmem(128, 1024), vmem(64, 1024),
            vmem(16, 1024, dtype=jnp.int32), vmem(8, 1024, dtype=jnp.int32),
            vmem(4, 256, 1024), vmem(2, 1024, 256), vmem(8, 1024, dtype=jnp.int32),
            vmem(2, 144, 2048), vmem(2, 64, 2048), vmem(2, 128, 4096), vmem(2, 64, 4096),
            vmem(2, 128, HALF, dtype=F32), vmem(2, 144, HALF, dtype=F32), vmem(2, 64, HALF, dtype=F32),
            vmem(2, 128, HALF), vmem(2, 64, HALF), vmem(2, 32, HALF),
            vmem(2, 128, HALF), vmem(2, 64, HALF), vmem(2, 32, HALF),
            pltpu.SemaphoreType.DMA((15,)), pltpu.SemaphoreType.DMA((6,)),
            pltpu.SemaphoreType.DMA((21,)), pltpu.SemaphoreType.DMA((21,)),
            pltpu.SemaphoreType.DMA((7, 3, 3)), pltpu.SemaphoreType.DMA((7, 3, 3)),
        ],
        compiler_params=pltpu.CompilerParams(
            collective_id=0, has_side_effects=True, vmem_limit_bytes=56 << 20
        ),
        cost_estimate=pl.CostEstimate(flops=7 * 10**9, bytes_accessed=10 << 20, transcendentals=0),
        name="sweeps",
    )(*args)


def solution(mesh):
    split = P("leaf", "panel", None)
    return jax.shard_map(
        body,
        mesh=mesh,
        in_specs=(split,) * 13 + (P(), P()),
        out_specs=(split,) * 6,
        check_vma=False,
    )
```

time: 585 us -> 101 us (0.17)
  waiting for transfers between devices: 364 us -> 0 us
  blocking collectives: 98.2 us -> 0 us
  Pallas kernels: 0 us -> 93.9 us
  other arithmetic: 50.5 us -> 0 us
  starting transfers between devices: 30.1 us -> 0 us
  matrix products: 13.8 us -> 0 us
  between operations: 14 us -> 0.67 us
  local copies, waits for them, and re-layouts: 13.4 us -> 4.81 us
    all_gather x3 -> x0, waiting for transfers between devices: 183 us -> none  [collect(): whole = lax.all_gather(piece, 'panel', axis=1, tiled=True)]
    ppermute x9 -> x0, waiting for transfers between devices: 181 us -> none  [from_partner(): return lax.ppermute(value, axis, pairs)]
    all_gather x4 -> x0, blocking collectives: 98.2 us -> none  [collect(): whole = lax.all_gather(piece, 'panel', axis=1, tiled=True)]
    pallas_call x0 -> x1, Pallas kernels: none -> 93.9 us  [body(): pl.pallas_call(kernel, out_shape=tuple((jax.ShapeDtypeStruct((1, n, 256),...]
    scatter-add x4 -> x0, other arithmetic: 37.2 us -> none  [the longest x2 20.8 us: child_total(): return total.at[other_map].add(other.astype(jnp.float32))]
    ppermute x9 -> x0, starting transfers between devices: 29.9 us -> none  [from_partner(): return lax.ppermute(value, axis, pairs)]
    dot_general x10 -> x0, matrix products: 13.8 us -> none  [product(): return jnp.dot(matrix[0], rhs, preferred_element_type=jnp.float32)]
    gather x2 -> x0, local copies, waits for them, and re-layouts: 11.4 us -> none  [the longest x1 6.46 us: sweeps(): taken_mid = jnp.take(parent_top, map_mid, axis=0)]
  transfers between devices with their start and end apart: 12 -> 0, of which waited for: 12 -> 0; matrix products, arithmetic and copies ran while one was open for 4% -> 0% of each run, Pallas kernels for 0% -> 0%
where the time goes in v1:
time: 101 us; the launch traced here: 99.4 us
  Pallas kernels  93.9 us (93%)
  local copies, waits for them, and re-layouts  4.81 us (5%)
    pallas_call x1, Pallas kernels, body(): pl.pallas_call(kernel, out_shape=tuple((jax.ShapeDtypeStruct((1, n, 256),...  93.9 us
    unnamed x16, local copies, waits for them, and re-layouts  4.81 us

profile of v1, /device:TPU:1, one launch (start us, length us, event | category | flops | bytes accessed | tf_op | source)
XLA Modules:
  0.0 99.4 jit_solution(6839059111591814408)
XLA Ops:
  0.6 93.9 %sweeps.1 = (bf16[1,128,256]{2,1,0:T(8,128)(2,1)}, bf16[1,64,256]{2,1,0:T(8,128)(2,1)}, bf16[1,32,256]{2,1,0:T(8,128)(2,1)}, bf16[1,128,256]{2,1,0:T(8,128)(2,1)...) custom-call(bf16[1,128,256]{2,1,0:T(8,128)(2,1)} %probe_low.1, bf16[1,64,256]{2,1,0:T(8,128)(2,1)} %probe_mid.1, ...), custom_call_target="tpu_custom_call" | custom-call | flops 7000000000 | bytes 10485760 | tf_op jit(solution)/shard_map/sweeps/pallas_call | solution.py:395
  94.6 0.0 copy-start.2
  94.6 0.0 copy-start.4
  94.6 1.5 %copy.27 = bf16[1,128,256]{2,1,0:T(8,128)(2,1)} copy(bf16[1,128,256]{2,1,0:T(8,128)(2,1)} %get-tuple-element.12) | data formatting | bytes 131072
  96.1 0.0 copy-done.2
  96.1 0.0 copy-start
  96.1 0.6 copy.28
  96.7 0.0 copy-done.4
  96.7 0.6 copy.29
  97.3 0.0 copy-done
  97.3 0.0 copy-start.1
  97.3 0.6 copy.30
  98.0 0.1 copy-done.1
  98.1 0.0 copy-start.3
  98.1 0.6 copy.31
  98.7 0.1 copy-done.3
  98.8 0.6 copy.32
Async XLA Ops:
  94.6 1.5 %copy-start.2 = (bf16[1,64,256]{2,1,0:T(8,128)(2,1)S(1)}, bf16[1,64,256]{2,1,0:T(8,128)(2,1)}, u32[]{:S(2)}) copy-start(bf16[1,64,256]{2,1,0:T(8,128)(2,1)} %get-tuple-element.13) | copy-start | bytes 98308
  94.6 2.1 %copy-start.4 = (bf16[1,32,256]{2,1,0:T(8,128)(2,1)S(1)}, bf16[1,32,256]{2,1,0:T(8,128)(2,1)}, u32[]{:S(2)}) copy-start(bf16[1,32,256]{2,1,0:T(8,128)(2,1)} %get-tuple-element.14) | copy-start | bytes 49156
  96.1 1.2 %copy-start = (bf16[1,128,256]{2,1,0:T(8,128)(2,1)S(1)}, bf16[1,128,256]{2,1,0:T(8,128)(2,1)}, u32[]{:S(2)}) copy-start(bf16[1,128,256]{2,1,0:T(8,128)(2,1)} %get-tuple-element.15) | copy-start | bytes 196612
  97.3 0.8 copy-start.1
  98.1 0.7 copy-start.3

commit v2 on v1

v2 whole, which is shorter than its diff:
```python
import jax
import jax.numpy as jnp
from jax import lax
from jax.experimental import pallas as pl
from jax.experimental.pallas import tpu as pltpu
from jax.sharding import PartitionSpec as P

MESH = pl.DeviceIdType.MESH
BF16, F32 = jnp.bfloat16, jnp.float32
HALF = 128
COPIES = 192


def kernel(
    probe_low, probe_mid, probe_top, inv_low, inv_mid, inv_top, gram_low, gram_mid, gram_top,
    panel_low, panel_mid, back_low, back_mid, sep_low, sep_mid,
    half_low, half_mid, half_top, solved_low, solved_mid, solved_top,
    d_rl, d_ul, d_um, d_st, d_sm, d_pm, d_pt,
    m_pl, m_low, m_mid, m_top, b_low, b_mid, s_low, s_mid, onehot, onehot_t, high,
    q_mid, qg_top, qh_top, c_low, c_mid, acc_low, acc_mid, g_mid, pg_top, ph_top,
    o_hl, o_hm, o_ht, o_sl, o_sm, o_st,
    load_sem, out_sem, send_sem, recv_sem,
):
    z = lax.axis_index("leaf")
    p = lax.axis_index("panel")
    c = lax.rem(p, 2)
    x = lax.rem(p // 2, 4)
    y = p // 8
    z2, z4 = lax.rem(z, 2), lax.rem(z, 4)
    cols = pl.ds(pl.multiple_of(c * HALF, HALF), HALF)
    other_cols = pl.ds(pl.multiple_of((1 - c) * HALF, HALF), HALF)

    def place(d, e, core=c):
        return x ^ jnp.where(core == 0, d, e), y ^ jnp.where(core == 0, e, d)

    def device(d=0, e=0, dz=0, core=c):
        xx, yy = place(d, e, core)
        return {"leaf": z ^ dz, "panel": (yy * 4 + xx) * 2 + core}

    sibling = {"leaf": z, "panel": p + 1 - 2 * c}

    def rows(count):
        return pl.ds(pl.multiple_of(c * count, count), count)

    def other(count):
        return pl.ds(pl.multiple_of((1 - c) * count, count), count)

    n_loads = [0]

    def load(src, dst):
        copy = pltpu.make_async_copy(src, dst, load_sem.at[n_loads[0]])
        n_loads[0] += 1
        copy.start()
        return copy

    own = [
        load(probe_low.at[0, :, cols], d_rl.at[0, y, x, rows(128)]),
        load(probe_mid.at[0, :, cols], d_pm.at[z2, y, x, rows(64)]),
        load(probe_top.at[0, :, cols], d_pt.at[z4, y, x, rows(32)]),
    ]
    load_sep = [load(sep_low, s_low), load(sep_mid, s_mid)]
    load_mid = [
        load(panel_mid.at[0], m_mid.at[c, 0:16]),
        load(inv_mid.at[0], m_mid.at[c, 16:80]),
        load(gram_mid.at[0], m_mid.at[c, 80:144]),
    ]
    load_top = [load(gram_top.at[0], m_top.at[c, 0:32]), load(inv_top.at[0], m_top.at[c, 32:64])]
    load_pl = load(panel_low.at[0], m_pl.at[c])
    load_back = [load(back_low.at[0], b_low), load(back_mid.at[0], b_mid.at[z2])]
    load_low = [load(inv_low.at[0], m_low.at[c, 0]), load(gram_low.at[0], m_low.at[c, 1])]

    barrier = pltpu.get_barrier_semaphore()
    partners = [sibling]
    for d in (1, 2, 3):
        partners += [device(d), device(0, d), device(dz=d), device(d, dz=1)]
        partners += [device(d, core=1 - c), device(0, d, core=1 - c)]
    for partner in partners:
        pl.semaphore_signal(barrier, 1, device_id=partner, device_id_type=MESH)
    pl.semaphore_wait(barrier, len(partners))

    n_sent = [0]
    unsent = []

    def send(src, dst, to, arriving=None):
        i = n_sent[0]
        n_sent[0] += 1
        copy = pltpu.make_async_remote_copy(
            src, dst, send_sem.at[i], recv_sem.at[i], device_id=to, device_id_type=MESH
        )
        copy.start()
        unsent.append(copy)
        if arriving is None:
            arriving = dst

        def wait():
            pltpu.make_async_remote_copy(
                arriving, arriving, send_sem.at[i], recv_sem.at[i], device_id=to, device_id_type=MESH
            ).wait_recv()

        return wait

    def drain():
        for copy in unsent:
            copy.wait_send()
        unsent.clear()

    def all_of(waits):
        for wait in waits:
            wait()

    def swap(src, buf, *at):
        return send(src, buf.at[(c, *at)], sibling, buf.at[(1 - c, *at)])

    def swap_probe(src, buf, zz, n):
        return send(
            src.at[0, :, other_cols], buf.at[zz, y, x, rows(n)], sibling, buf.at[zz, y, x, other(n)]
        )

    class Gather:
        def __init__(self, buf):
            self.buf, self.first, self.second = buf, {1: [], 2: [], 3: [], 0: []}, []

        def part(self, d, e, zz=slice(None)):
            xx, yy = place(d, e)
            return self.buf.at[zz, yy, xx]

        def begin(self, zz=slice(None)):
            for d in (1, 3, 2):
                self.first[d].append(
                    send(self.part(0, 0, zz), self.part(0, 0, zz), device(d), self.part(d, 0, zz))
                )

        def begin_pair(self):
            here, there = z2, 1 - z2
            for d, dz in ((1, 0), (3, 0), (0, 1), (1, 1), (3, 1), (2, 0), (2, 1)):
                self.first[d].append(
                    send(
                        self.part(0, 0, here), self.part(0, 0, here), device(d, dz=dz),
                        self.part(d, 0, there if dz else here),
                    )
                )

        def planes(self, offsets, here):
            self.z = [
                (here ^ d, send(self.part(0, 0, here), self.part(0, 0, here), device(dz=d), self.part(0, 0, here ^ d)))
                for d in offsets
            ]

        def relay(self):
            for zz, wait in self.z:
                wait()
                for d in (1, 3, 2):
                    self.first[d].append(
                        send(self.part(0, 0, zz), self.part(0, 0, zz), device(d), self.part(d, 0, zz))
                    )

        def forward(self, *offsets):
            for d in offsets:
                all_of(self.first[d])
                for e in (1, 3, 2):
                    self.second.append(
                        send(self.part(d, 0), self.part(d, 0), device(0, e), self.part(d, e))
                    )

        def finish(self):
            all_of(self.second)

    def dot(a, b):
        return jnp.dot(a, b, preferred_element_type=F32)

    def whole(buf):
        return buf[...].reshape(-1, HALF)

    def tables(first, count):
        for i in range(first, first + count):
            table, row = (s_low, (z - z2) + i) if i < 2 else (s_mid, 2 * (z // 4) + i - 2)
            sep = table[pl.ds(row, 1), :]
            high[i : i + 1, :] = lax.shift_right_logical(sep, 8)
            low = jnp.bitwise_and(sep, 255)
            for j in range(4):
                at = slice(j * 256, (j + 1) * 256)
                grid = lax.broadcasted_iota(jnp.int32, (256, 256), 0)
                hot = jnp.where(grid == low[:, at], 1.0, 0.0)
                onehot[i, :, at] = hot.astype(BF16)

    def own_tables():
        for i, (table, row) in enumerate(((s_low, z), (s_mid, z // 2))):
            sep = table[pl.ds(row, 1), :]
            high[4 + i : 5 + i, :] = lax.shift_right_logical(sep, 8)
            low = jnp.bitwise_and(sep, 255)
            for j in range(4):
                at = slice(j * 256, (j + 1) * 256)
                grid = lax.broadcasted_iota(jnp.int32, (256, 256), 0)
                hot = jnp.where(grid == low[:, at], 1.0, 0.0)
                onehot_t[i, at, :] = hot.T.astype(BF16)

    def take_columns(src, start, dst, i, total, block):
        at0 = (i % 2) * 1024

        def step(r, _):
            value = src[c, pl.ds(pl.multiple_of(start + r * block, 16), block), :]
            tall = jnp.concatenate([value[:, k * 256 : (k + 1) * 256] for k in range(16)], 0)
            part = pl.ds(pl.multiple_of(r * block, 16), block)
            for j in range(4):
                at = slice(j * 256, (j + 1) * 256)
                found = dot(tall, onehot[i, :, at])
                which = high[i : i + 1, at]
                picked = jnp.zeros((block, 256), F32)
                for k in range(16):
                    picked = jnp.where(which == k, found[k * block : (k + 1) * block], picked)
                dst[part, at0 + j * 256 : at0 + (j + 1) * 256] = picked.astype(BF16)
            return 0

        lax.fori_loop(0, total // block, step, 0)

    def spread_columns(src, dst, i, total, block):
        def step(r, _):
            part = pl.ds(pl.multiple_of(r * block, block), block)
            value = src[part, :]
            which = high[4 + i : 5 + i, :]
            tall = jnp.concatenate(
                [value * jnp.where(which == k, 1.0, 0.0).astype(BF16) for k in range(16)], 0
            )
            found = dot(tall, onehot_t[i])
            for k in range(16):
                dst[part, k * 256 : (k + 1) * 256] = found[k * block : (k + 1) * block].astype(BF16)
            return 0

        lax.fori_loop(0, total // block, step, 0)

    given = []

    def give(out, buf):
        copy = pltpu.make_async_copy(buf.at[c], out.at[0, :, cols], out_sem.at[len(given)])
        copy.start()
        given.append((copy, send(buf.at[1 - c], out.at[0, :, cols], sibling, out.at[0, :, other_cols])))

    right_low = Gather(d_rl)
    mine = d_rl.at[0, y, x, rows(128)]
    for d in (1, 3, 2):
        xx, yy = place(d, 0)
        right_low.first[d].append(
            send(probe_low.at[0, :, cols], mine, device(d), d_rl.at[0, yy, xx, rows(128)])
        )
        right_low.first[d].append(
            send(probe_low.at[0, :, other_cols], mine, device(d, core=1 - c), d_rl.at[0, yy, xx, other(128)])
        )
    right_low.first[0].append(swap_probe(probe_low, d_rl, 0, 128))
    in_pm = swap_probe(probe_mid, d_pm, z2, 64)
    in_pt = swap_probe(probe_top, d_pt, z4, 32)
    in_back = send(back_mid.at[0], b_mid.at[z2], device(dz=1), b_mid.at[1 - z2])
    own[1].wait()
    in_pm()
    pm = Gather(d_pm)
    pm.planes((1,), z2)
    pm.begin(z2)
    own[2].wait()
    in_pt()
    pt = Gather(d_pt)
    pt.planes((1, 2, 3), z4)
    own[0].wait()
    right_low.forward(0)
    in_pl = swap(panel_low.at[0], m_pl)
    all_of([copy.wait for copy in load_sep])
    tables(2, 2)
    all_of([copy.wait for copy in load_top])
    take_columns(m_top, 0, qg_top.at[z4, c], 2, 32, 32)
    take_columns(m_top, 0, qg_top.at[z4, c], 3, 32, 32)
    piece = qg_top.at[z4, c]
    z_qg = [(d, send(piece, piece, device(dz=d), qg_top.at[z4 ^ d, c])) for d in (1, 2, 3)]
    right_low.forward(1, 3)
    pm.relay()
    right_low.forward(2)
    in_qg = [send(piece, piece, sibling, qg_top.at[z4, 1 - c])]
    in_mid = [
        swap(panel_mid.at[0], m_mid, slice(0, 16)),
        swap(inv_mid.at[0], m_mid, slice(16, 80)),
        swap(gram_mid.at[0], m_mid, slice(80, 144)),
    ]
    in_low = [swap(inv_low.at[0], m_low, 0), swap(gram_low.at[0], m_low, 1)]
    in_top = [swap(gram_top.at[0], m_top, slice(0, 32)), swap(inv_top.at[0], m_top, slice(32, 64))]
    tables(0, 2)
    all_of([copy.wait for copy in load_mid])
    take_columns(m_mid, 0, q_mid.at[c], 0, 144, 48)
    take_columns(m_mid, 0, q_mid.at[c], 1, 144, 48)
    in_q_mid = swap(q_mid.at[c], q_mid)
    pm.forward(0, 1, 3, 2)
    load_pl.wait()
    in_pl()
    right_low.finish()
    d_ul[z2, y, x] = dot(m_pl[...].reshape(64, 4096), whole(d_rl)).astype(BF16)

    update_low = Gather(d_ul)
    update_low.begin_pair()
    pt.begin(z4)
    pt.relay()
    own_tables()
    all_of([copy.wait for copy in load_back])
    in_back()
    spread_columns(b_mid.at[z2], c_mid.at[z2, c], 1, 64, 32)
    update_low.forward(0, 1, 3, 2)
    pt.forward(0, 1, 3, 2)
    spread_columns(b_mid.at[1 - z2], c_mid.at[1 - z2, c], 1, 64, 32)
    in_c_mid = [
        send(c_mid.at[zz, c], c_mid.at[zz, c], sibling, c_mid.at[zz, 1 - c]) for zz in (0, 1)
    ]
    drain()
    all_of(in_mid)
    pm.finish()
    acc_mid[...] = dot(m_mid[...].reshape(288, 4096), whole(d_pm)).reshape(2, 144, HALF)
    in_q_mid()
    update_low.finish()
    update = acc_mid[:, 0:16].reshape(32, HALF) - dot(q_mid[:, 0:16].reshape(32, 2048), whole(d_ul))
    d_um[z4, y, x] = update.astype(BF16)

    update_mid = Gather(d_um)
    update_mid.planes((1, 2, 3), z4)
    update_mid.begin(z4)
    result = acc_mid[:, 16:144] - dot(q_mid[:, 16:144].reshape(256, 2048), whole(d_ul)).reshape(2, 128, HALF)
    o_hm[...] = result[:, 0:64].astype(BF16)
    g_mid[z2] = result[:, 64:128]
    update_mid.relay()
    in_g_mid = send(g_mid.at[z2], g_mid.at[z2], device(dz=1), g_mid.at[1 - z2])
    give(half_mid, o_hm)
    for d, wait in z_qg:
        wait()
        piece = qg_top.at[z4 ^ d, c]
        in_qg.append(send(piece, piece, sibling, qg_top.at[z4 ^ d, 1 - c]))
    all_of([copy.wait for copy in load_low])
    all_of(in_low)
    result = dot(m_low[...].reshape(512, 4096), whole(d_rl)).reshape(2, 2, 128, HALF)
    o_hl[...] = result[:, 0].astype(BF16)
    acc_low[...] = result[:, 1]
    update_mid.forward(0, 1, 3, 2)
    give(half_low, o_hl)
    all_of(in_top)
    pt.finish()
    result = dot(m_top[...].reshape(128, 4096), whole(d_pt)).reshape(2, 64, HALF)
    pg_top[z4] = result[:, 0:32]
    ph_top[...] = result[:, 32:64]
    in_pg = [send(pg_top.at[z4], pg_top.at[z4], device(dz=d), pg_top.at[z4 ^ d]) for d in (1, 2, 3)]
    drain()
    take_columns(m_top, 32, qh_top.at[c], 2, 32, 32)
    take_columns(m_top, 32, qh_top.at[c], 3, 32, 32)
    in_qh = swap(qh_top.at[c], qh_top)
    all_of(in_qg)
    all_of(in_pg)
    update_mid.finish()
    top = (pg_top[...].reshape(256, HALF) - dot(qg_top[...].reshape(256, 2048), whole(d_um))).astype(BF16)
    d_st[:, y, x] = top.reshape(4, 64, HALF)

    top_rows = Gather(d_st)
    top_rows.begin()
    spread_columns(b_low, c_low.at[c], 0, 128, 32)
    in_c_low = swap(c_low.at[c], c_low)
    top_rows.forward(0, 1, 3, 2)
    o_st[...] = d_st[z4, y, x].reshape(2, 32, HALF)
    give(solved_top, o_st)
    in_qh()
    o_ht[...] = (ph_top[...] - dot(qh_top[...].reshape(64, 2048), whole(d_um)).reshape(2, 32, HALF)).astype(BF16)
    give(half_top, o_ht)
    drain()
    in_g_mid()
    all_of(in_c_mid)
    top_rows.finish()
    mid = (g_mid[...].reshape(256, HALF) - dot(c_mid[...].reshape(256, 4096), whole(d_st))).astype(BF16)
    d_sm[:, y, x] = mid.reshape(2, 128, HALF)
    mid_rows = Gather(d_sm)
    mid_rows.begin()
    mid_rows.forward(0, 1, 3, 2)
    o_sm[...] = d_sm[z2, y, x].reshape(2, 64, HALF)
    give(solved_mid, o_sm)
    for copy, wait in given:
        copy.wait()
        wait()
    n_given = len(given)
    in_c_low()
    drain()
    mid_rows.finish()
    result = acc_low[...] - dot(c_low[...].reshape(256, 4096), whole(d_sm)).reshape(2, 128, HALF)
    o_sl[...] = result.astype(BF16)
    give(solved_low, o_sl)
    for copy, wait in given[n_given:]:
        copy.wait()
        wait()
    drain()


def hand_over(*refs):
    ins, outs, held, sems = refs[:6], refs[6:12], refs[12:18], refs[18]
    first = [pltpu.make_async_copy(a, b, sems.at[i, 0]) for i, (a, b) in enumerate(zip(ins, held))]
    second = [pltpu.make_async_copy(a, b, sems.at[i, 1]) for i, (a, b) in enumerate(zip(held, outs))]
    for copy in first:
        copy.start()
    for one, two in zip(first, second):
        one.wait()
        two.start()
    for copy in second:
        copy.wait()


def body(*args):
    shapes = (128, 64, 32, 128, 64, 32)

    def vmem(*shape, dtype=BF16):
        return pltpu.VMEM(shape, dtype)

    results = tuple(jax.ShapeDtypeStruct((1, n, 256), BF16) for n in shapes)
    anywhere = pl.BlockSpec(memory_space=pl.ANY)
    found = pl.pallas_call(
        kernel,
        out_shape=results,
        in_specs=[anywhere] * 15,
        out_specs=(anywhere,) * 6,
        scratch_shapes=[
            vmem(1, 4, 4, 256, HALF), vmem(2, 4, 4, 64, HALF), vmem(4, 4, 4, 32, HALF), vmem(4, 4, 4, 64, HALF),
            vmem(2, 4, 4, 128, HALF), vmem(2, 4, 4, 128, HALF), vmem(4, 4, 4, 64, HALF),
            vmem(2, 32, 4096), vmem(2, 2, 128, 4096), vmem(2, 144, 4096), vmem(2, 64, 4096),
            vmem(128, 1024), vmem(2, 64, 1024),
            vmem(16, 1024, dtype=jnp.int32), vmem(8, 1024, dtype=jnp.int32),
            vmem(4, 256, 1024), vmem(2, 1024, 256), vmem(8, 1024, dtype=jnp.int32),
            vmem(2, 144, 2048), vmem(4, 2, 32, 2048), vmem(2, 32, 2048), vmem(2, 128, 4096), vmem(2, 2, 64, 4096),
            vmem(2, 128, HALF, dtype=F32), vmem(2, 144, HALF, dtype=F32), vmem(2, 2, 64, HALF, dtype=F32),
            vmem(4, 2, 32, HALF, dtype=F32), vmem(2, 32, HALF, dtype=F32),
            vmem(2, 128, HALF), vmem(2, 64, HALF), vmem(2, 32, HALF),
            vmem(2, 128, HALF), vmem(2, 64, HALF), vmem(2, 32, HALF),
            pltpu.SemaphoreType.DMA((15,)), pltpu.SemaphoreType.DMA((6,)),
            pltpu.SemaphoreType.DMA((COPIES,)), pltpu.SemaphoreType.DMA((COPIES,)),
        ],
        compiler_params=pltpu.CompilerParams(
            collective_id=0, has_side_effects=True, vmem_limit_bytes=56 << 20
        ),
        cost_estimate=pl.CostEstimate(flops=7 * 10**9, bytes_accessed=10 << 20, transcendentals=0),
        name="sweeps",
    )(*args)
    return pl.pallas_call(
        hand_over,
        out_shape=results,
        in_specs=[anywhere] * 6,
        out_specs=(anywhere,) * 6,
        scratch_shapes=[vmem(1, n, 256) for n in shapes] + [pltpu.SemaphoreType.DMA((6, 2))],
        name="hand_over",
    )(*found)


def solution(mesh):
    split = P("leaf", "panel", None)
    return jax.shard_map(
        body,
        mesh=mesh,
        in_specs=(split,) * 13 + (P(), P()),
        out_specs=(split,) * 6,
        check_vma=False,
    )
```

time: 101 us -> 87.4 us (0.87); the launches traced: 99.4 us -> 87.2 us
  Pallas kernels: 93.9 us -> 86.6 us
  local copies, waits for them, and re-layouts: 4.81 us -> 0 us
    pallas_call x1 -> x2, Pallas kernels: 93.9 us -> 86.6 us  [the longest x1 84.9 us: body(): pl.pallas_call(kernel, out_shape=results, in_specs=[anywhere] * 15, out_s...]
    unnamed x16 -> x0, local copies, waits for them, and re-layouts: 4.81 us -> none
where the time goes in v2:
time: 87.4 us; the launch traced here: 87.2 us
  Pallas kernels  86.6 us (99%)
    pallas_call x1, Pallas kernels, body(): pl.pallas_call(kernel, out_shape=results, in_specs=[anywhere] * 15, out_s...  84.9 us

profile of v2, /device:TPU:1, one launch (start us, length us, event | category | flops | bytes accessed | tf_op | source)
XLA Modules:
  0.0 87.2 jit_solution(5339005448863285638)
XLA Ops:
  0.6 84.9 %sweeps.1 = (bf16[1,128,256]{2,1,0:T(8,128)(2,1)}, bf16[1,64,256]{2,1,0:T(8,128)(2,1)}, bf16[1,32,256]{2,1,0:T(8,128)(2,1)}, bf16[1,128,256]{2,1,0:T(8,128)(2,1)...) custom-call(bf16[1,128,256]{2,1,0:T(8,128)(2,1)} %probe_low.1, bf16[1,64,256]{2,1,0:T(8,128)(2,1)} %probe_mid.1, ...), custom_call_target="tpu_custom_call" | custom-call | flops 7000000000 | bytes 10485760 | tf_op jit(solution)/shard_map/sweeps/pallas_call | solution.py:410
  85.6 1.7 %hand_over.1 = (bf16[1,128,256]{2,1,0:T(8,128)(2,1)}, bf16[1,64,256]{2,1,0:T(8,128)(2,1)}, bf16[1,32,256]{2,1,0:T(8,128)(2,1)}, bf16[1,128,256]{2,1,0:T(8,128)(2...) custom-call(bf16[1,128,256]{2,1,0:T(8,128)(2,1)} %get-tuple-element.12.refs_0_, ...), custom_call_target="tpu_custom_call" | custom-call | tf_op jit(solution)/shard_map/hand_over/pallas_call | solution.py:436

commit v3 on v2

--- a/solution.py
+++ b/solution.py
@@ -268,9 +268,8 @@
     take_columns(m_top, 0, qg_top.at[z4, c], 3, 32, 32)
     piece = qg_top.at[z4, c]
     z_qg = [(d, send(piece, piece, device(dz=d), qg_top.at[z4 ^ d, c])) for d in (1, 2, 3)]
-    right_low.forward(1, 3)
+    right_low.forward(1, 3, 2)
     pm.relay()
-    right_low.forward(2)
     in_qg = [send(piece, piece, sibling, qg_top.at[z4, 1 - c])]
     in_mid = [
         swap(panel_mid.at[0], m_mid, slice(0, 16)),
@@ -287,8 +286,14 @@
     pm.forward(0, 1, 3, 2)
     load_pl.wait()
     in_pl()
-    right_low.finish()
-    d_ul[z2, y, x] = dot(m_pl[...].reshape(64, 4096), whole(d_rl)).astype(BF16)
+    update = jnp.zeros((64, HALF), F32)
+    for k, d in enumerate((0, 1, 3, 2)):
+        all_of(right_low.second[3 * k : 3 * k + 3])
+        for e in range(4):
+            xx, yy = place(d, e)
+            at = pl.ds(pl.multiple_of((yy * 4 + xx) * 256, 256), 256)
+            update += dot(m_pl[:, :, at].reshape(64, 256), d_rl[0, yy, xx])
+    d_ul[z2, y, x] = update.astype(BF16)
 
     update_low = Gather(d_ul)
     update_low.begin_pair()
@@ -299,7 +304,6 @@
     in_back()
     spread_columns(b_mid.at[z2], c_mid.at[z2, c], 1, 64, 32)
     update_low.forward(0, 1, 3, 2)
-    pt.forward(0, 1, 3, 2)
     spread_columns(b_mid.at[1 - z2], c_mid.at[1 - z2, c], 1, 64, 32)
     in_c_mid = [
         send(c_mid.at[zz, c], c_mid.at[zz, c], sibling, c_mid.at[zz, 1 - c]) for zz in (0, 1)
@@ -309,6 +313,7 @@
     pm.finish()
     acc_mid[...] = dot(m_mid[...].reshape(288, 4096), whole(d_pm)).reshape(2, 144, HALF)
     in_q_mid()
+    pt.forward(0, 1, 3, 2)
     update_low.finish()
     update = acc_mid[:, 0:16].reshape(32, HALF) - dot(q_mid[:, 0:16].reshape(32, 2048), whole(d_ul))
     d_um[z4, y, x] = update.astype(BF16)

time: 87.4 us -> 80.4 us (0.920)
  Pallas kernels: 86.6 us -> 79.6 us
    pallas_call x1, Pallas kernels: 84.9 us -> 78 us  [body(): pl.pallas_call(kernel, out_shape=results, in_specs=[anywhere] * 15, out_s...]
where the time goes in v3:
time: 80.4 us; the launch traced here: 80.3 us
  Pallas kernels  79.6 us (99%)
    pallas_call x1, Pallas kernels, body(): pl.pallas_call(kernel, out_shape=results, in_specs=[anywhere] * 15, out_s...  78 us
    pallas_call x1, Pallas kernels, body(): pl.pallas_call(hand_over, out_shape=results, in_specs=[anywhere] * 6, out...  1.65 us

profile of v3, /device:TPU:1, one launch (start us, length us, event | category | flops | bytes accessed | tf_op | source)
XLA Modules:
  0.0 80.3 jit_solution(6389484019741983568)
XLA Ops:
  0.6 78.0 %sweeps.1 = (bf16[1,128,256]{2,1,0:T(8,128)(2,1)}, bf16[1,64,256]{2,1,0:T(8,128)(2,1)}, bf16[1,32,256]{2,1,0:T(8,128)(2,1)}, bf16[1,128,256]{2,1,0:T(8,128)(2,1)...) custom-call(bf16[1,128,256]{2,1,0:T(8,128)(2,1)} %probe_low.1, bf16[1,64,256]{2,1,0:T(8,128)(2,1)} %probe_mid.1, ...), custom_call_target="tpu_custom_call" | custom-call | flops 7000000000 | bytes 10485760 | tf_op jit(solution)/shard_map/sweeps/pallas_call | solution.py:415
  78.6 1.7 %hand_over.1 = (bf16[1,128,256]{2,1,0:T(8,128)(2,1)}, bf16[1,64,256]{2,1,0:T(8,128)(2,1)}, bf16[1,32,256]{2,1,0:T(8,128)(2,1)}, bf16[1,128,256]{2,1,0:T(8,128)(2...) custom-call(bf16[1,128,256]{2,1,0:T(8,128)(2,1)} %get-tuple-element.12.refs_0_, ...), custom_call_target="tpu_custom_call" | custom-call | tf_op jit(solution)/shard_map/hand_over/pallas_call | solution.py:441
